TPU v7x, 512 devices: a whole 4x4x16 slice. The times are simulated.
512 devices in a mesh: lat: 16 (over x, y_hi, core), lon: 32 (over z, y_lo).
Axes of the slice: x: 4, y: 4 (y_hi: 2, y_lo: 2; y = y_hi * 2 + y_lo), z: 16, core: 2. Of those that a mesh axis runs over, the one named last changes fastest.
Arguments:
- tracer: float32 [8, 256, 36864], P(None, 'lat', 'lon'), may hold values from -6 to 6
- flux: float32 [256, 36864], P('lat', 'lon'), may hold values from -6 to 6
- winds: float32 [3, 8, 256, 768], P(None, None, 'lat', 'lon'), may hold values from -0.3 to 0.3
- obs_cells: int32 [8192, 3], P(('lat', 'lon')), may hold values from 0 to 767, as said below
- obs_count: int32 [512], P(('lat', 'lon')), may hold values from 1 to 16, as said below
- obs_value: float32 [8192], P(('lat', 'lon')), may hold values from -6 to 6
- obs_var: float32 [8192], P(('lat', 'lon')), may hold values from 21.333334 to 341.33334
Outputs:
- tracer_out: float32 [8, 256, 36864], P(None, 'lat', 'lon')
- flux_out: float32 [256, 36864], P('lat', 'lon')
Inputs may be any that keep to these rules, and one draw needn't show every extreme that they name: `obs_cells`: slot k lies in the block of 16 slots of device k div 16 (devices in lat-major order), and its cell lies in that device's block of the grid: row in its 16 rows, column in its 24 columns, level below 8. Each device's first slot is the last row, last column and highest level of its block, its second slot the first row, first column and level 0 of its block. Cells may repeat. Live slots are the first obs_count of each device's slots; some device has all 16 slots live.
All inputs are finite; a program needn't handle non-finite values.
Results may differ from a plain program's by a relative error of at most 0.0001.
Values sent between devices are 32-bit elements; how exact they have to be, the bound alone decides.
A program may use at most 64 MiB of HBM per device.

v0:
```python
import jax
import jax.numpy as jnp
from jax import lax
from jax.sharding import PartitionSpec as P

M = 48
NS_ITERS = 5
KH = 0.15


def with_halo(value, sides, width, wrap):
    for axis, dim in sides:
        size, length = (lax.axis_size(axis), value.shape[dim])
        up = [(i, (i + 1) % size) for i in range(size if wrap else size - 1)]
        down = [(j, i) for i, j in up]
        last = lax.slice_in_dim(value, length - width, length, axis=dim)
        leading = lax.slice_in_dim(value, 0, width, axis=dim)
        before = lax.ppermute(last, axis, up)
        after = lax.ppermute(leading, axis, down)
        value = jnp.concatenate([before, value, after], axis=dim)
    return value


def advance(center, lat_minus, lat_plus, lon_prev, lon_next, wind_u, wind_v, wind_w):
    zeros = jnp.zeros_like(center[:1])
    above = jnp.concatenate([center[1:], zeros], axis=0)
    below = jnp.concatenate([zeros, center[:-1]], axis=0)
    result = (
        center - 0.5 * wind_u * (lon_next - lon_prev) + KH * (lon_next - 2.0 * center + lon_prev)
    )
    result = (
        result - 0.5 * wind_v * (lat_plus - lat_minus) + KH * (lat_plus - 2.0 * center + lat_minus)
    )
    result = result - 0.5 * wind_w * (above - below) + KH * (above - 2.0 * center + below)
    return result


def member_transform(gram, proj, members):
    eye = jnp.eye(members, dtype=jnp.float32)
    hp = lax.Precision.HIGHEST
    system = (members - 1.0) * eye + gram
    scale = jnp.sqrt(jnp.sum(system * system))
    root_now = system / scale
    inverse_now = eye
    for step in range(NS_ITERS):
        factor = 0.5 * (3.0 * eye - jnp.dot(inverse_now, root_now, precision=hp))
        root_now = jnp.dot(root_now, factor, precision=hp)
        inverse_now = jnp.dot(factor, inverse_now, precision=hp)
    wmean = jnp.dot(inverse_now, jnp.dot(inverse_now, proj, precision=hp), precision=hp) / scale
    root = jnp.sqrt((members - 1.0) / scale) * inverse_now
    centering = eye - 1.0 / members
    return jnp.dot(centering, wmean[:, None] + root, precision=hp) + 1.0 / members


def as_members(flat, columns):
    return flat.reshape(flat.shape[0], flat.shape[1], columns, M)


def advance_flat(center, lat_minus, lat_plus, lon_prev, lon_next, wind_block):
    columns = wind_block.shape[-1]
    result = advance(
        as_members(center, columns),
        as_members(lat_minus, columns),
        as_members(lat_plus, columns),
        as_members(lon_prev, columns),
        as_members(lon_next, columns),
        wind_block[0][..., None],
        wind_block[1][..., None],
        wind_block[2][..., None],
    )
    return result.reshape(center.shape)


def shallow_step(field, winds):
    lon_wide = with_halo(field, (("lon", 2),), M, True)
    lat_wide = with_halo(field, (("lat", 1),), 1, False)
    return advance_flat(
        field,
        lat_wide[:, :-2],
        lat_wide[:, 2:],
        lon_wide[:, :, : -2 * M],
        lon_wide[:, :, 2 * M :],
        winds,
    )


def on_device(tracer, flux, winds, obs_cells, obs_count, obs_value, obs_var):
    hp = lax.Precision.HIGHEST
    levels, rows, width = tracer.shape
    columns = width // M
    field = tracer.at[0].add(flux)
    field = shallow_step(field, winds)
    field = shallow_step(field, winds)
    row_local = obs_cells[:, 0] - lax.axis_index("lat") * rows
    col_local = obs_cells[:, 1] - lax.axis_index("lon") * columns
    flat_index = (obs_cells[:, 2] * rows + row_local) * columns + col_local
    member_rows = field.reshape(-1, M)
    observed = jnp.take(member_rows, flat_index, axis=0)
    slots = obs_value.shape[0]
    live = (jnp.arange(slots, dtype=jnp.int32) < obs_count[0]).astype(jnp.float32)
    hbar = jnp.mean(observed, axis=1)
    anomalies = observed - hbar[:, None]
    weight = live / obs_var
    weighted_innov = weight * (obs_value - hbar)
    gram_part = jnp.dot(anomalies.T * weight[None, :], anomalies, precision=hp)
    proj_part = jnp.dot(anomalies.T, weighted_innov, precision=hp)
    gram, proj = lax.psum((gram_part, proj_part), ("lat", "lon"))
    mixing = member_transform(gram, proj, M)
    tracer_out = jnp.dot(member_rows, mixing, precision=hp).reshape(levels, rows, width)
    flux_out = jnp.dot(flux.reshape(-1, M), mixing, precision=hp).reshape(rows, width)
    return (tracer_out, flux_out)


def solution(mesh):
    return jax.shard_map(
        on_device,
        mesh=mesh,
        in_specs=(
            P(None, "lat", "lon"),
            P("lat", "lon"),
            P(None, None, "lat", "lon"),
            P(("lat", "lon"), None),
            P(("lat", "lon")),
            P(("lat", "lon")),
            P(("lat", "lon")),
        ),
        out_specs=(P(None, "lat", "lon"), P("lat", "lon")),
        check_vma=False,
    )
```

profile of v0, /device:TPU:1, one launch (start us, length us, event | category | flops | bytes accessed | tf_op | source)
XLA Modules:
  0.0 195.2 jit_solution(5435071610383970742)
XLA Ops:
  0.6 1.1 copy.15
  1.7 0.9 fusion.14
  2.6 0.6 fusion.55
  3.3 13.0 %collective-permute-start = (f32[8,16,48]{2,1,0:T(8,128)}, f32[8,16,48]{2,1,0:T(8,128)S(1)}, u32[]{:S(2)}, u32[]{:S(2)}) collective-permute-start(f32[8,16,48]{2,1,0:T(8,128)} %get-tuple-element.32), channel_id=1, source_target_pairs={{1,0},{2,1},{3,2},{4,3},{5,4},{6,5},{7,6},{8,7},{9,8},{10,9},{11,1... | collective-permute-start | bytes 73736 | tf_op jit(solution)/shard_map/ppermute | solution.py:19
  16.2 1.9 collective-permute-start.1
  18.2 0.7 fusion.56
  18.9 2.9 %collective-permute-start.2 = (f32[8,1,1152]{2,1,0:T(1,128)}, f32[8,1,1152]{2,1,0:T(1,128)}, u32[]{:S(2)}, u32[]{:S(2)}) collective-permute-start(f32[8,1,1152]{2,1,0:T(1,128)} %get-tuple-element.34), channel_id=1, source_target_pairs={{32,0},{64,32},{96,64},{128,96},{160,128},{192,160},{224,192},{256... | collective-permute-start | bytes 110600 | tf_op jit(solution)/shard_map/ppermute | solution.py:19
  21.7 4.4 %collective-permute-start.3 = (f32[8,1,1152]{2,1,0:T(1,128)}, f32[8,1,1152]{2,1,0:T(1,128)}, u32[]{:S(2)}, u32[]{:S(2)}) collective-permute-start(f32[8,1,1152]{2,1,0:T(1,128)} %get-tuple-element.35), channel_id=1, source_target_pairs={{0,32},{32,64},{64,96},{96,128},{128,160},{160,192},{192,224},{224... | collective-permute-start | bytes 110600 | tf_op jit(solution)/shard_map/ppermute | solution.py:18
  26.1 0.9 fusion.57
  27.1 0.7 reshape.115
  28.0 2.8 %slice.130 = f32[7,16,24,48]{3,2,1,0:T(8,128)} reshape(f32[7,16,1152]{2,1,0:T(8,128)} %get-tuple-element.36) | data formatting | bytes 1032192 | tf_op jit(solution)/shard_map/slice | solution.py:26
  30.8 1.7 slice.132
  33.2 2.4 %pad_maximum_fusion.7 = (f32[8,16,1152]{2,1,0:T(8,128)}, f32[8,16,1152]{2,1,0:T(8,128)}, f32[8,16,1152]{2,1,0:T(8,128)}, f32[8,16,1152]{2,1,0:T(8,128)S(1)}) fusion(f32[8,16,48]{2,1,0:T(8,128)S(1)} %collective-permute-done, f32[8,16,1152]{2,1,0:T(8,128)S(1)} %fusion.14, f32[8,16,48]{2,1,0:T(8,128)S(1)} %collective-permute-done.1, ...), kind=kLoop, calls=%fused_computation.38 | loop fusion | flops 589824 | bytes 3072000 | tf_op jit(solution)/shard_map/concatenate | solution.py:20
  35.5 2.9 %reshape.116 = f32[8,16,24,48]{3,2,1,0:T(8,128)} reshape(f32[8,16,1152]{2,1,0:T(8,128)} %get-tuple-element.28) | data formatting | bytes 1179648 | tf_op jit(solution)/shard_map/reshape | solution.py:56
  38.4 2.9 %reshape.117 = f32[8,16,24,48]{3,2,1,0:T(8,128)} reshape(f32[8,16,1152]{2,1,0:T(8,128)} %get-tuple-element.29) | data formatting | bytes 1179648 | tf_op jit(solution)/shard_map/reshape | solution.py:56
  41.4 1.8 reshape.118
  43.2 1.8 reshape.119
  45.0 4.8 %fusion.2 = f32[8,16,24,48]{3,2,1,0:T(8,128)S(1)} fusion(f32[7,16,24,48]{3,2,1,0:T(8,128)} %slice.132, f32[7,16,24,48]{3,2,1,0:T(8,128)} %slice.130, f32[8,16,24,48]{3,2,1,0:T(8,128)} %reshape.119, f32[8,16,24,48]{3,2,1,0:T(8,128)} %reshape.118, f32[8,16,24,48]{3,2,1,0:T(8,128)} %reshape.117, f32[8,16,24,48]{3,2,1,0:T(8,128)} %reshape.116, ...), kind=kLoop, calls=%fused_computation.9 | loop fusion | flops 3244032 | bytes 4608000 | tf_op jit(solution)/shard_map/add | solution.py:34
  49.8 0.5 reshape.120
  50.5 5.2 %collective-permute-start.4 = (f32[8,16,48]{2,1,0:T(8,128)S(1)}, f32[8,16,48]{2,1,0:T(8,128)S(1)}, u32[]{:S(2)}, u32[]{:S(2)}) collective-permute-start(f32[8,16,48]{2,1,0:T(8,128)S(1)} %get-tuple-element.24), channel_id=1, source_target_pairs={{1,0},{2,1},{3,2},{4,3},{5,4},{6,5},{7,6},{8,7},{9,8},{10,9},{11,1... | collective-permute-start | bytes 73736 | tf_op jit(solution)/shard_map/ppermute | solution.py:19
  55.7 1.9 collective-permute-start.5
  57.7 1.9 collective-permute-start.6
  59.6 5.1 %collective-permute-start.7 = (f32[8,1,1152]{2,1,0:T(1,128)S(1)}, f32[8,1,1152]{2,1,0:T(1,128)S(1)}, u32[]{:S(2)}, u32[]{:S(2)}) collective-permute-start(f32[8,1,1152]{2,1,0:T(1,128)S(1)} %get-tuple-element.27), channel_id=1, source_target_pairs={{0,32},{32,64},{64,96},{96,128},{128,160},{160,192},{192,224},{224... | collective-permute-start | bytes 110600 | tf_op jit(solution)/shard_map/ppermute | solution.py:18
  64.7 1.8 fusion.52
  66.6 1.4 pad_maximum_fusion.3
  68.0 2.9 %reshape.121 = f32[8,16,24,48]{3,2,1,0:T(8,128)} reshape(f32[8,16,1152]{2,1,0:T(8,128)} %get-tuple-element.20) | data formatting | bytes 1179648 | tf_op jit(solution)/shard_map/reshape | solution.py:56
  70.9 1.8 reshape.122
  72.7 1.8 reshape.123
  74.6 1.8 reshape.124
  76.4 4.8 %fusion.6 = f32[8,16,24,48]{3,2,1,0:T(8,128)S(1)} fusion(f32[7,16,24,48]{3,2,1,0:T(8,128)} %get-tuple-element.19, f32[7,16,24,48]{3,2,1,0:T(8,128)} %get-tuple-element.18, f32[8,16,24,48]{3,2,1,0:T(8,128)} %reshape.124, f32[8,16,24,48]{3,2,1,0:T(8,128)} %reshape.123, f32[8,16,24,48]{3,2,1,0:T(8,128)} %reshape.122, f32[8,16,24,48]{3,2,1,0:T(8,128)} %reshape.121, ...), kind=kLoop, calls=%fused_computation.13 | loop fusion | flops 3244032 | bytes 4608000 | tf_op jit(solution)/shard_map/add | solution.py:34
  81.2 0.6 gather_fusion
  81.8 0.2 select_reduce_fusion
  82.0 0.3 fusion.25
  82.3 0.2 convolution_bitcast_fusion.3
  82.5 104.5 %all-reduce.4 = (f32[48,48]{1,0:T(8,128)S(1)}, f32[48]{0:T(128)S(1)}) all-reduce(f32[48,48]{1,0:T(8,128)S(1)} %fusion.25, f32[48]{0:T(128)S(1)} %convolution_bitcast_fusion.3), channel_id=1, replica_groups=mesh['lat'=16,'lon'=32] {'lat','lon'}, use_global_device_ids=true, to_apply=%region_1.2 | all-reduce | flops 2352 | bytes 18816 | tf_op jit(solution)/shard_map/psum | solution.py:107
  187.0 0.6 multiply_reduce_fusion
  188.8 0.2 fusion.11
  189.1 0.1 fusion.58
  189.2 0.2 fusion.10
  189.7 0.2 fusion.9
  190.2 0.2 fusion.8
  190.5 0.1 convolution_bitcast_fusion.2
  190.7 0.2 fusion.13
  191.0 0.2 convolution_add_fusion
  191.2 1.4 fusion.65
  192.6 1.3 reshape.125
  193.9 0.4 convolution_bitcast_fusion
  194.4 0.8 reshape.127
  (51 shorter events, 1.9 us)
Async XLA Ops:
  1.7 25.3 %copy-start.9 = (f32[3,8,16,24]{3,2,1,0:T(8,128)S(1)}, f32[3,8,16,24]{3,2,1,0:T(8,128)}, u32[]{:S(2)}) copy-start(f32[3,8,16,24]{3,2,1,0:T(8,128)} %param.11) | copy-start | bytes 110596
  1.7 25.4 %copy-start.10 = (s32[16,3]{0,1:T(4,128)S(1)}, s32[16,3]{0,1:T(4,128)}, u32[]{:S(2)}) copy-start(s32[16,3]{0,1:T(4,128)} %param.12) | copy-start | bytes 580
  3.3 29.9 %collective-permute-start = (f32[8,16,48]{2,1,0:T(8,128)}, f32[8,16,48]{2,1,0:T(8,128)S(1)}, u32[]{:S(2)}, u32[]{:S(2)}) collective-permute-start(f32[8,16,48]{2,1,0:T(8,128)} %get-tuple-element.32), channel_id=1, source_target_pairs={{1,0},{2,1},{3,2},{4,3},{5,4},{6,5},{7,6},{8,7},{9,8},{10,9},{11,1... | collective-permute-start | bytes 73736 | tf_op jit(solution)/shard_map/ppermute | solution.py:19
  16.2 16.9 %collective-permute-start.1 = (f32[8,16,48]{2,1,0:T(8,128)S(1)}, f32[8,16,48]{2,1,0:T(8,128)S(1)}, u32[]{:S(2)}, u32[]{:S(2)}) collective-permute-start(f32[8,16,48]{2,1,0:T(8,128)S(1)} %get-tuple-element.33), channel_id=1, source_target_pairs={{0,1},{1,2},{2,3},{3,4},{4,5},{5,6},{6,7},{7,8},{8,9},{9,10},{10,1... | collective-permute-start | bytes 73736 | tf_op jit(solution)/shard_map/ppermute | solution.py:18
  18.9 14.3 %collective-permute-start.2 = (f32[8,1,1152]{2,1,0:T(1,128)}, f32[8,1,1152]{2,1,0:T(1,128)}, u32[]{:S(2)}, u32[]{:S(2)}) collective-permute-start(f32[8,1,1152]{2,1,0:T(1,128)} %get-tuple-element.34), channel_id=1, source_target_pairs={{32,0},{64,32},{96,64},{128,96},{160,128},{192,160},{224,192},{256... | collective-permute-start | bytes 110600 | tf_op jit(solution)/shard_map/ppermute | solution.py:19
  21.7 11.4 %collective-permute-start.3 = (f32[8,1,1152]{2,1,0:T(1,128)}, f32[8,1,1152]{2,1,0:T(1,128)}, u32[]{:S(2)}, u32[]{:S(2)}) collective-permute-start(f32[8,1,1152]{2,1,0:T(1,128)} %get-tuple-element.35), channel_id=1, source_target_pairs={{0,32},{32,64},{64,96},{96,128},{128,160},{160,192},{192,224},{224... | collective-permute-start | bytes 110600 | tf_op jit(solution)/shard_map/ppermute | solution.py:18
  27.0 0.9 copy-start.8
  27.0 18.0 %copy-start.2 = (f32[8,16,24]{2,1,0:T(8,128)}, f32[8,16,24]{2,1,0:T(8,128)S(1)}, u32[]{:S(2)}) copy-start(f32[8,16,24]{2,1,0:T(8,128)S(1)} %get-tuple-element.38) | copy-start | bytes 36868
  27.0 18.0 %copy-start.4 = (f32[8,16,24]{2,1,0:T(8,128)}, f32[8,16,24]{2,1,0:T(8,128)S(1)}, u32[]{:S(2)}) copy-start(f32[8,16,24]{2,1,0:T(8,128)S(1)} %get-tuple-element.39) | copy-start | bytes 36868
  27.1 18.0 %copy-start.6 = (f32[8,16,24]{2,1,0:T(8,128)}, f32[8,16,24]{2,1,0:T(8,128)S(1)}, u32[]{:S(2)}) copy-start(f32[8,16,24]{2,1,0:T(8,128)S(1)} %get-tuple-element.40) | copy-start | bytes 36868
  38.4 2.9 %copy-start = (f32[8,16,1152]{2,1,0:T(8,128)S(1)}, f32[8,16,1152]{2,1,0:T(8,128)}, u32[]{:S(2)}) copy-start(f32[8,16,1152]{2,1,0:T(8,128)} %get-tuple-element.30) | copy-start | bytes 1769476
  50.5 16.1 %collective-permute-start.4 = (f32[8,16,48]{2,1,0:T(8,128)S(1)}, f32[8,16,48]{2,1,0:T(8,128)S(1)}, u32[]{:S(2)}, u32[]{:S(2)}) collective-permute-start(f32[8,16,48]{2,1,0:T(8,128)S(1)} %get-tuple-element.24), channel_id=1, source_target_pairs={{1,0},{2,1},{3,2},{4,3},{5,4},{6,5},{7,6},{8,7},{9,8},{10,9},{11,1... | collective-permute-start | bytes 73736 | tf_op jit(solution)/shard_map/ppermute | solution.py:19
  55.7 10.8 %collective-permute-start.5 = (f32[8,16,48]{2,1,0:T(8,128)S(1)}, f32[8,16,48]{2,1,0:T(8,128)S(1)}, u32[]{:S(2)}, u32[]{:S(2)}) collective-permute-start(f32[8,16,48]{2,1,0:T(8,128)S(1)} %get-tuple-element.25), channel_id=1, source_target_pairs={{0,1},{1,2},{2,3},{3,4},{4,5},{5,6},{6,7},{7,8},{8,9},{9,10},{10,1... | collective-permute-start | bytes 73736 | tf_op jit(solution)/shard_map/ppermute | solution.py:18
  57.7 8.9 %collective-permute-start.6 = (f32[8,1,1152]{2,1,0:T(1,128)S(1)}, f32[8,1,1152]{2,1,0:T(1,128)S(1)}, u32[]{:S(2)}, u32[]{:S(2)}) collective-permute-start(f32[8,1,1152]{2,1,0:T(1,128)S(1)} %get-tuple-element.26), channel_id=1, source_target_pairs={{32,0},{64,32},{96,64},{128,96},{160,128},{192,160},{224,192},{256... | collective-permute-start | bytes 110600 | tf_op jit(solution)/shard_map/ppermute | solution.py:19
  59.6 7.0 %collective-permute-start.7 = (f32[8,1,1152]{2,1,0:T(1,128)S(1)}, f32[8,1,1152]{2,1,0:T(1,128)S(1)}, u32[]{:S(2)}, u32[]{:S(2)}) collective-permute-start(f32[8,1,1152]{2,1,0:T(1,128)S(1)} %get-tuple-element.27), channel_id=1, source_target_pairs={{0,32},{32,64},{64,96},{96,128},{128,160},{160,192},{192,224},{224... | collective-permute-start | bytes 110600 | tf_op jit(solution)/shard_map/ppermute | solution.py:18
  68.0 2.9 %copy-start.1 = (f32[8,16,1152]{2,1,0:T(8,128)S(1)}, f32[8,16,1152]{2,1,0:T(8,128)}, u32[]{:S(2)}) copy-start(f32[8,16,1152]{2,1,0:T(8,128)} %get-tuple-element.21) | copy-start | bytes 1769476
  74.5 1.8 copy-start.3
  74.5 1.8 copy-start.5
  74.5 1.8 copy-start.7
  76.4 5.6 %copy-start.11 = (f32[16]{0:T(128)S(1)}, f32[16]{0:T(128)}, u32[]{:S(2)}) copy-start(f32[16]{0:T(128)} %param.15) | copy-start | bytes 196
  76.4 5.9 %copy-start.12 = (f32[16]{0:T(128)S(1)}, f32[16]{0:T(128)}, u32[]{:S(2)}) copy-start(f32[16]{0:T(128)} %param.14) | copy-start | bytes 196
where the time goes:
time: 196 us; the launch traced here: 195 us
  blocking collectives  105 us (54%)
  starting transfers between devices  36.4 us (19%)
  local copies, waits for them, and re-layouts  31.7 us (16%)
  other arithmetic  15.1 us (8%)
  matrix products  4.89 us (2%)
  between operations  2.51 us (1%)
    psum x1, blocking collectives, on_device(): gram, proj = lax.psum((gram_part, proj_part), ('lat', 'lon'))  105 us
    ppermute x4, starting transfers between devices, with_halo(): after = lax.ppermute(leading, axis, down)  23 us
    reshape x9, local copies, waits for them, and re-layouts, as_members(): return flat.reshape(flat.shape[0], flat.shape[1], columns, M)  18.5 us
    ppermute x4, starting transfers between devices, with_halo(): before = lax.ppermute(last, axis, up)  13.4 us
    add x2, other arithmetic, advance(): result - 0.5 * wind_w * (above - below)  9.61 us
    slice x3, local copies, waits for them, and re-layouts, advance(): above = jnp.concatenate([center[1:], zeros], axis=0)  5.45 us
  transfers between devices with their start and end apart: 8, of which 0 were waited for; matrix products, arithmetic and copies ran while one was open for 4% of the time, Pallas kernels for 0%

commit v1 on v0

--- a/solution.py
+++ b/solution.py
@@ -104,7 +104,7 @@
     weighted_innov = weight * (obs_value - hbar)
     gram_part = jnp.dot(anomalies.T * weight[None, :], anomalies, precision=hp)
     proj_part = jnp.dot(anomalies.T, weighted_innov, precision=hp)
-    gram, proj = lax.psum((gram_part, proj_part), ("lat", "lon"))
+    gram, proj = lax.psum(lax.psum((gram_part, proj_part), "lon"), "lat")
     mixing = member_transform(gram, proj, M)
     tracer_out = jnp.dot(member_rows, mixing, precision=hp).reshape(levels, rows, width)
     flux_out = jnp.dot(flux.reshape(-1, M), mixing, precision=hp).reshape(rows, width)

time: 196 us -> 275 us (1.40)
  blocking collectives: 105 us -> 182 us
    psum x1 -> x2, blocking collectives: 105 us -> 182 us  [on_device(): gram, proj = lax.psum(lax.psum((gram_part, proj_part), 'lon'), 'lat')]
  transfers between devices with their start and end apart: 8 -> 8, of which waited for: 0 -> 0; matrix products, arithmetic and copies ran while one was open for 4% -> 3% of each run, Pallas kernels for 0% -> 0%
where the time goes in v1:
time: 275 us; the launch traced here: 273 us
  blocking collectives  182 us (66%)
  starting transfers between devices  36.4 us (13%)
  local copies, waits for them, and re-layouts  31.8 us (12%)
  other arithmetic  15.2 us (6%)
  matrix products  4.88 us (2%)
    psum x2, blocking collectives, on_device(): gram, proj = lax.psum(lax.psum((gram_part, proj_part), 'lon'), 'lat')  182 us
    ppermute x4, starting transfers between devices, with_halo(): after = lax.ppermute(leading, axis, down)  23 us
    reshape x9, local copies, waits for them, and re-layouts, as_members(): return flat.reshape(flat.shape[0], flat.shape[1], columns, M)  18.5 us
    ppermute x4, starting transfers between devices, with_halo(): before = lax.ppermute(last, axis, up)  13.4 us
    add x2, other arithmetic, advance(): result - 0.5 * wind_w * (above - below)  9.68 us
    slice x3, local copies, waits for them, and re-layouts, advance(): above = jnp.concatenate([center[1:], zeros], axis=0)  5.5 us
  transfers between devices with their start and end apart: 8, of which 0 were waited for; matrix products, arithmetic and copies ran while one was open for 3% of the time, Pallas kernels for 0%

profile of v1, /device:TPU:1, one launch (start us, length us, event | category | flops | bytes accessed | tf_op | source)
XLA Modules:
  0.0 272.7 jit_solution(6633827818572718030)
XLA Ops:
  0.6 1.1 copy.15
  1.7 0.9 fusion.14
  2.6 0.6 fusion.55
  3.3 13.0 %collective-permute-start = (f32[8,16,48]{2,1,0:T(8,128)}, f32[8,16,48]{2,1,0:T(8,128)S(1)}, u32[]{:S(2)}, u32[]{:S(2)}) collective-permute-start(f32[8,16,48]{2,1,0:T(8,128)} %get-tuple-element.34), channel_id=1, source_target_pairs={{1,0},{2,1},{3,2},{4,3},{5,4},{6,5},{7,6},{8,7},{9,8},{10,9},{11,1... | collective-permute-start | bytes 73736 | tf_op jit(solution)/shard_map/ppermute | solution.py:19
  16.2 1.9 collective-permute-start.1
  18.2 0.7 fusion.56
  18.9 2.9 %collective-permute-start.2 = (f32[8,1,1152]{2,1,0:T(1,128)}, f32[8,1,1152]{2,1,0:T(1,128)}, u32[]{:S(2)}, u32[]{:S(2)}) collective-permute-start(f32[8,1,1152]{2,1,0:T(1,128)} %get-tuple-element.36), channel_id=1, source_target_pairs={{32,0},{64,32},{96,64},{128,96},{160,128},{192,160},{224,192},{256... | collective-permute-start | bytes 110600 | tf_op jit(solution)/shard_map/ppermute | solution.py:19
  21.7 4.4 %collective-permute-start.3 = (f32[8,1,1152]{2,1,0:T(1,128)}, f32[8,1,1152]{2,1,0:T(1,128)}, u32[]{:S(2)}, u32[]{:S(2)}) collective-permute-start(f32[8,1,1152]{2,1,0:T(1,128)} %get-tuple-element.37), channel_id=1, source_target_pairs={{0,32},{32,64},{64,96},{96,128},{128,160},{160,192},{192,224},{224... | collective-permute-start | bytes 110600 | tf_op jit(solution)/shard_map/ppermute | solution.py:18
  26.2 0.9 fusion.57
  27.1 0.7 reshape.115
  28.0 2.8 %slice.130 = f32[7,16,24,48]{3,2,1,0:T(8,128)} reshape(f32[7,16,1152]{2,1,0:T(8,128)} %get-tuple-element.38) | data formatting | bytes 1032192 | tf_op jit(solution)/shard_map/slice | solution.py:26
  30.8 1.7 slice.132
  33.2 2.4 pad_maximum_fusion.7
  35.6 2.9 %reshape.116 = f32[8,16,24,48]{3,2,1,0:T(8,128)} reshape(f32[8,16,1152]{2,1,0:T(8,128)} %get-tuple-element.30) | data formatting | bytes 1179648 | tf_op jit(solution)/shard_map/reshape | solution.py:56
  38.4 2.9 %reshape.117 = f32[8,16,24,48]{3,2,1,0:T(8,128)} reshape(f32[8,16,1152]{2,1,0:T(8,128)} %get-tuple-element.31) | data formatting | bytes 1179648 | tf_op jit(solution)/shard_map/reshape | solution.py:56
  41.4 1.8 reshape.118
  43.2 1.8 reshape.119
  45.0 4.8 %fusion.2 = f32[8,16,24,48]{3,2,1,0:T(8,128)S(1)} fusion(f32[7,16,24,48]{3,2,1,0:T(8,128)} %slice.132, f32[7,16,24,48]{3,2,1,0:T(8,128)} %slice.130, f32[8,16,24,48]{3,2,1,0:T(8,128)} %reshape.119, f32[8,16,24,48]{3,2,1,0:T(8,128)} %reshape.118, f32[8,16,24,48]{3,2,1,0:T(8,128)} %reshape.117, f32[8,16,24,48]{3,2,1,0:T(8,128)} %reshape.116, ...), kind=kLoop, calls=%fused_computation.9 | loop fusion | flops 3244032 | bytes 4608000 | tf_op jit(solution)/shard_map/add | solution.py:34
  49.9 0.5 reshape.120
  50.5 5.2 %collective-permute-start.4 = (f32[8,16,48]{2,1,0:T(8,128)S(1)}, f32[8,16,48]{2,1,0:T(8,128)S(1)}, u32[]{:S(2)}, u32[]{:S(2)}) collective-permute-start(f32[8,16,48]{2,1,0:T(8,128)S(1)} %get-tuple-element.26), channel_id=1, source_target_pairs={{1,0},{2,1},{3,2},{4,3},{5,4},{6,5},{7,6},{8,7},{9,8},{10,9},{11,1... | collective-permute-start | bytes 73736 | tf_op jit(solution)/shard_map/ppermute | solution.py:19
  55.8 1.9 collective-permute-start.5
  57.7 1.9 collective-permute-start.6
  59.6 5.1 %collective-permute-start.7 = (f32[8,1,1152]{2,1,0:T(1,128)S(1)}, f32[8,1,1152]{2,1,0:T(1,128)S(1)}, u32[]{:S(2)}, u32[]{:S(2)}) collective-permute-start(f32[8,1,1152]{2,1,0:T(1,128)S(1)} %get-tuple-element.29), channel_id=1, source_target_pairs={{0,32},{32,64},{64,96},{96,128},{128,160},{160,192},{192,224},{224... | collective-permute-start | bytes 110600 | tf_op jit(solution)/shard_map/ppermute | solution.py:18
  64.8 1.8 fusion.52
  66.7 1.4 pad_maximum_fusion.3
  68.1 2.9 %reshape.121 = f32[8,16,24,48]{3,2,1,0:T(8,128)} reshape(f32[8,16,1152]{2,1,0:T(8,128)} %get-tuple-element.22) | data formatting | bytes 1179648 | tf_op jit(solution)/shard_map/reshape | solution.py:56
  71.0 1.8 reshape.122
  72.9 1.8 reshape.123
  74.7 1.8 reshape.124
  76.5 4.8 %fusion.6 = f32[8,16,24,48]{3,2,1,0:T(8,128)S(1)} fusion(f32[7,16,24,48]{3,2,1,0:T(8,128)} %get-tuple-element.21, f32[7,16,24,48]{3,2,1,0:T(8,128)} %get-tuple-element.20, f32[8,16,24,48]{3,2,1,0:T(8,128)} %reshape.124, f32[8,16,24,48]{3,2,1,0:T(8,128)} %reshape.123, f32[8,16,24,48]{3,2,1,0:T(8,128)} %reshape.122, f32[8,16,24,48]{3,2,1,0:T(8,128)} %reshape.121, ...), kind=kLoop, calls=%fused_computation.13 | loop fusion | flops 3244032 | bytes 4608000 | tf_op jit(solution)/shard_map/add | solution.py:34
  81.4 0.6 gather_fusion
  81.9 0.2 select_reduce_fusion
  82.1 0.3 fusion.25
  82.4 0.2 convolution_bitcast_fusion.3
  82.6 94.6 %all-reduce.4 = (f32[48,48]{1,0:T(8,128)S(1)}, f32[48]{0:T(128)S(1)}) all-reduce(f32[48,48]{1,0:T(8,128)S(1)} %fusion.25, f32[48]{0:T(128)S(1)} %convolution_bitcast_fusion.3), channel_id=1, replica_groups=mesh['lat'=16,'lon'=32] {'lon'}, use_global_device_ids=true, to_apply=%region_1.2 | all-reduce | flops 2352 | bytes 18816 | tf_op jit(solution)/shard_map/psum | solution.py:107
  177.2 87.4 %all-reduce.5 = (f32[48,48]{1,0:T(8,128)S(1)}, f32[48]{0:T(128)S(1)}) all-reduce(f32[48,48]{1,0:T(8,128)S(1)} %get-tuple-element.14, f32[48]{0:T(128)S(1)} %get-tuple-element.15), channel_id=1, replica_groups=mesh['lat'=16,'lon'=32] {'lat'}, use_global_device_ids=true, to_apply=%region_2.3 | all-reduce | flops 2352 | bytes 18816 | tf_op jit(solution)/shard_map/psum | solution.py:107
  264.6 0.6 multiply_reduce_fusion
  266.4 0.2 fusion.11
  266.8 0.2 fusion.10
  267.3 0.2 fusion.9
  267.6 0.1 fusion.62
  267.8 0.2 fusion.8
  268.3 0.2 fusion.13
  268.5 0.2 convolution_add_fusion
  268.8 1.4 fusion.65
  270.1 1.3 reshape.125
  271.4 0.4 convolution_bitcast_fusion
  272.0 0.8 reshape.127
  (52 shorter events, 2.1 us)
Async XLA Ops:
  1.7 25.3 %copy-start.9 = (f32[3,8,16,24]{3,2,1,0:T(8,128)S(1)}, f32[3,8,16,24]{3,2,1,0:T(8,128)}, u32[]{:S(2)}) copy-start(f32[3,8,16,24]{3,2,1,0:T(8,128)} %param.11) | copy-start | bytes 110596
  1.7 25.4 %copy-start.10 = (s32[16,3]{0,1:T(4,128)S(1)}, s32[16,3]{0,1:T(4,128)}, u32[]{:S(2)}) copy-start(s32[16,3]{0,1:T(4,128)} %param.12) | copy-start | bytes 580
  3.3 29.9 %collective-permute-start = (f32[8,16,48]{2,1,0:T(8,128)}, f32[8,16,48]{2,1,0:T(8,128)S(1)}, u32[]{:S(2)}, u32[]{:S(2)}) collective-permute-start(f32[8,16,48]{2,1,0:T(8,128)} %get-tuple-element.34), channel_id=1, source_target_pairs={{1,0},{2,1},{3,2},{4,3},{5,4},{6,5},{7,6},{8,7},{9,8},{10,9},{11,1... | collective-permute-start | bytes 73736 | tf_op jit(solution)/shard_map/ppermute | solution.py:19
  16.2 16.9 %collective-permute-start.1 = (f32[8,16,48]{2,1,0:T(8,128)S(1)}, f32[8,16,48]{2,1,0:T(8,128)S(1)}, u32[]{:S(2)}, u32[]{:S(2)}) collective-permute-start(f32[8,16,48]{2,1,0:T(8,128)S(1)} %get-tuple-element.35), channel_id=1, source_target_pairs={{0,1},{1,2},{2,3},{3,4},{4,5},{5,6},{6,7},{7,8},{8,9},{9,10},{10,1... | collective-permute-start | bytes 73736 | tf_op jit(solution)/shard_map/ppermute | solution.py:18
  18.9 14.3 %collective-permute-start.2 = (f32[8,1,1152]{2,1,0:T(1,128)}, f32[8,1,1152]{2,1,0:T(1,128)}, u32[]{:S(2)}, u32[]{:S(2)}) collective-permute-start(f32[8,1,1152]{2,1,0:T(1,128)} %get-tuple-element.36), channel_id=1, source_target_pairs={{32,0},{64,32},{96,64},{128,96},{160,128},{192,160},{224,192},{256... | collective-permute-start | bytes 110600 | tf_op jit(solution)/shard_map/ppermute | solution.py:19
  21.7 11.5 %collective-permute-start.3 = (f32[8,1,1152]{2,1,0:T(1,128)}, f32[8,1,1152]{2,1,0:T(1,128)}, u32[]{:S(2)}, u32[]{:S(2)}) collective-permute-start(f32[8,1,1152]{2,1,0:T(1,128)} %get-tuple-element.37), channel_id=1, source_target_pairs={{0,32},{32,64},{64,96},{96,128},{128,160},{160,192},{192,224},{224... | collective-permute-start | bytes 110600 | tf_op jit(solution)/shard_map/ppermute | solution.py:18
  27.0 0.9 copy-start.8
  27.0 18.0 %copy-start.2 = (f32[8,16,24]{2,1,0:T(8,128)}, f32[8,16,24]{2,1,0:T(8,128)S(1)}, u32[]{:S(2)}) copy-start(f32[8,16,24]{2,1,0:T(8,128)S(1)} %get-tuple-element.40) | copy-start | bytes 36868
  27.0 18.0 %copy-start.4 = (f32[8,16,24]{2,1,0:T(8,128)}, f32[8,16,24]{2,1,0:T(8,128)S(1)}, u32[]{:S(2)}) copy-start(f32[8,16,24]{2,1,0:T(8,128)S(1)} %get-tuple-element.41) | copy-start | bytes 36868
  27.1 18.0 %copy-start.6 = (f32[8,16,24]{2,1,0:T(8,128)}, f32[8,16,24]{2,1,0:T(8,128)S(1)}, u32[]{:S(2)}) copy-start(f32[8,16,24]{2,1,0:T(8,128)S(1)} %get-tuple-element.42) | copy-start | bytes 36868
  38.4 3.0 %copy-start = (f32[8,16,1152]{2,1,0:T(8,128)S(1)}, f32[8,16,1152]{2,1,0:T(8,128)}, u32[]{:S(2)}) copy-start(f32[8,16,1152]{2,1,0:T(8,128)} %get-tuple-element.32) | copy-start | bytes 1769476
  50.5 16.1 %collective-permute-start.4 = (f32[8,16,48]{2,1,0:T(8,128)S(1)}, f32[8,16,48]{2,1,0:T(8,128)S(1)}, u32[]{:S(2)}, u32[]{:S(2)}) collective-permute-start(f32[8,16,48]{2,1,0:T(8,128)S(1)} %get-tuple-element.26), channel_id=1, source_target_pairs={{1,0},{2,1},{3,2},{4,3},{5,4},{6,5},{7,6},{8,7},{9,8},{10,9},{11,1... | collective-permute-start | bytes 73736 | tf_op jit(solution)/shard_map/ppermute | solution.py:19
  55.8 10.9 %collective-permute-start.5 = (f32[8,16,48]{2,1,0:T(8,128)S(1)}, f32[8,16,48]{2,1,0:T(8,128)S(1)}, u32[]{:S(2)}, u32[]{:S(2)}) collective-permute-start(f32[8,16,48]{2,1,0:T(8,128)S(1)} %get-tuple-element.27), channel_id=1, source_target_pairs={{0,1},{1,2},{2,3},{3,4},{4,5},{5,6},{6,7},{7,8},{8,9},{9,10},{10,1... | collective-permute-start | bytes 73736 | tf_op jit(solution)/shard_map/ppermute | solution.py:18
  57.7 8.9 %collective-permute-start.6 = (f32[8,1,1152]{2,1,0:T(1,128)S(1)}, f32[8,1,1152]{2,1,0:T(1,128)S(1)}, u32[]{:S(2)}, u32[]{:S(2)}) collective-permute-start(f32[8,1,1152]{2,1,0:T(1,128)S(1)} %get-tuple-element.28), channel_id=1, source_target_pairs={{32,0},{64,32},{96,64},{128,96},{160,128},{192,160},{224,192},{256... | collective-permute-start | bytes 110600 | tf_op jit(solution)/shard_map/ppermute | solution.py:19
  59.6 7.0 %collective-permute-start.7 = (f32[8,1,1152]{2,1,0:T(1,128)S(1)}, f32[8,1,1152]{2,1,0:T(1,128)S(1)}, u32[]{:S(2)}, u32[]{:S(2)}) collective-permute-start(f32[8,1,1152]{2,1,0:T(1,128)S(1)} %get-tuple-element.29), channel_id=1, source_target_pairs={{0,32},{32,64},{64,96},{96,128},{128,160},{160,192},{192,224},{224... | collective-permute-start | bytes 110600 | tf_op jit(solution)/shard_map/ppermute | solution.py:18
  68.1 3.0 %copy-start.1 = (f32[8,16,1152]{2,1,0:T(8,128)S(1)}, f32[8,16,1152]{2,1,0:T(8,128)}, u32[]{:S(2)}) copy-start(f32[8,16,1152]{2,1,0:T(8,128)} %get-tuple-element.23) | copy-start | bytes 1769476
  74.7 1.8 copy-start.3
  74.7 1.8 copy-start.5
  74.7 1.8 copy-start.7
  76.5 5.6 %copy-start.11 = (f32[16]{0:T(128)S(1)}, f32[16]{0:T(128)}, u32[]{:S(2)}) copy-start(f32[16]{0:T(128)} %param.15) | copy-start | bytes 196
  76.5 5.9 %copy-start.12 = (f32[16]{0:T(128)S(1)}, f32[16]{0:T(128)}, u32[]{:S(2)}) copy-start(f32[16]{0:T(128)} %param.14) | copy-start | bytes 196
